TPU v7x, 32 devices: a whole 2x2x4 slice. The times are simulated.
32 devices in a mesh: shard: 8 (over z, y), dp: 4 (over x, core).
Axes of the slice: x: 2, y: 2, z: 4, core: 2. Of those that a mesh axis runs over, the one named last changes fastest.
Arguments:
- gate_up: bfloat16 [8192, 448], P(('shard', 'dp')), may hold values from -6 to 6
- route_weight: float32 [8192], P(('shard', 'dp')), may hold values from 0.1 to 1
- live_rows: int32 [32], P(('shard', 'dp')), may hold values from 1 to 256, 4915 in all
- down_weight: bfloat16 [4224, 224], P('shard'), may hold values from -0.375 to 0.375
- out_grad: bfloat16 [8192, 4224], P(('shard', 'dp')), may hold values from -6 to 6
Outputs:
- expert_out: bfloat16 [8192, 4224], P(('shard', 'dp'))
- grad_gate_up: bfloat16 [8192, 448], P(('shard', 'dp'))
- grad_route: float32 [8192], P(('shard', 'dp'))
- grad_down: float32 [4224, 224], P('shard')
Inputs may be any that keep to these rules, and one draw needn't show every extreme that they name: `live_rows`: at least one device uses all 256 slots.
All inputs are finite; a program needn't handle non-finite values.
Results may differ from a plain program's by a relative error of at most 0.005.
Values may be sent and summed in bfloat16 or wider, within the bound.
A program may use at most 64 MiB of HBM per device.

v0:
```python
import jax
import jax.numpy as jnp
from jax import lax
from jax.sharding import PartitionSpec as P


def per_device(gate_up, route_weight, live_rows, down_weight, out_grad):
    slot_count = gate_up.shape[0]
    hidden_units = gate_up.shape[1] // 2
    row_mask = (lax.iota(jnp.int32, slot_count) < live_rows[0]).astype(jnp.float32)[:, None]
    gate_pre = gate_up[:, :hidden_units].astype(jnp.float32)
    up_proj = gate_up[:, hidden_units:].astype(jnp.float32)
    sigmoid_gate = jax.nn.sigmoid(gate_pre)
    activated = gate_pre * sigmoid_gate
    hidden = (row_mask * activated * up_proj).astype(jnp.bfloat16)
    row_scale = route_weight[:, None]
    gathered = lax.all_gather(down_weight, "shard", axis=0, tiled=True)
    full = lax.dot_general(
        hidden, gathered, (((1,), (1,)), ((), ())), preferred_element_type=jnp.float32
    )
    expert_out = (row_scale * full).astype(jnp.bfloat16)
    grad_route = row_mask[:, 0] * jnp.sum(out_grad.astype(jnp.float32) * full, axis=1)
    grad_full = (row_mask * row_scale * out_grad.astype(jnp.float32)).astype(jnp.bfloat16)
    grad_hidden = jnp.dot(grad_full, gathered, preferred_element_type=jnp.float32)
    grad_gate = grad_hidden * up_proj * sigmoid_gate * (1.0 + gate_pre * (1.0 - sigmoid_gate))
    grad_up = grad_hidden * activated
    grad_gate_up = jnp.concatenate([grad_gate, grad_up], axis=1).astype(jnp.bfloat16)
    owned = lax.psum_scatter(
        lax.dot_general(
            grad_full, hidden, (((0,), (0,)), ((), ())), preferred_element_type=jnp.float32
        ),
        "shard",
        scatter_dimension=0,
        tiled=True,
    )
    grad_down = lax.psum(owned, "dp")
    return (expert_out, grad_gate_up, grad_route, grad_down)


def solution(mesh):
    in_specs = (
        P(("shard", "dp"), None),
        P(("shard", "dp")),
        P(("shard", "dp")),
        P("shard", None),
        P(("shard", "dp"), None),
    )
    out_specs = (
        P(("shard", "dp"), None),
        P(("shard", "dp"), None),
        P(("shard", "dp")),
        P("shard", None),
    )
    return jax.shard_map(
        per_device, mesh=mesh, in_specs=in_specs, out_specs=out_specs, check_vma=False
    )
```

profile of v0, /device:TPU:0, one launch (start us, length us, event | category | flops | bytes accessed | tf_op | source)
XLA Modules:
  0.0 198.6 jit_solution(15867833306919215617)
XLA Ops:
  7.2 0.0 all-gather.2.cloned.1.call-start
  7.2 0.7 all-gather.2.cloned.1.call-update
  7.9 0.0 reduce-scatter.2.cloned.1.call-start
  8.6 0.7 fusion.15
  9.3 4.5 %fusion.2 = f32[4224,224]{1,0:T(8,128)} fusion(bf16[256,4224]{1,0:T(8,128)(2,1)} %param.9, f32[256]{0:T(256)S(1)} %fusion.15, f32[256]{0:T(256)S(1)} %fusion.16, bf16[256,448]{0,1:T(8,128)(2,1)} %param.5), kind=kOutput, calls=%fused_computation.5 | convolution fusion | flops 488202240 | bytes 6178816 | tf_op jit(solution)/shard_map/dot_general | solution.py:29
  13.8 0.0 copy-start
  13.8 0.0 copy-start.1
  13.8 0.0 reduce-scatter.2.cloned.1.call-update
  13.8 0.0 copy-start.2
  13.9 0.0 all-reduce.2.cloned.1.call-start
  13.9 49.0 %all-gather.2.cloned.1.call-done = bf16[4224,224]{1,0:T(8,128)(2,1)} async-done(((bf16[528,224]{1,0:T(8,128)(2,1)}), bf16[4224,224]{1,0:T(8,128)(2,1)}) %all-gather.2.cloned.1.call-update) | async-done | bytes 1892368 | tf_op jit(solution)/shard_map/all_gather | solution.py:17
  62.9 0.0 copy-done
  62.9 0.0 copy-done.1
  62.9 0.0 copy-start.3
  62.9 3.0 %fusion.9 = (bf16[256,224]{0,1:T(8,128)(2,1)S(1)}, bf16[256,224]{0,1:T(8,128)(2,1)S(1)}) fusion(bf16[256,448]{0,1:T(8,128)(2,1)S(1)} %copy-done.1, bf16[4224,224]{1,0:T(8,128)(2,1)} %all-gather.2.cloned.1.call-done, bf16[256,4224]{1,0:T(8,128)(2,1)S(1)} %copy-done, f32[256]{0:T(256)S(1)} %fusion.15), kind=kOutput, calls=%fused_computation.15 | convolution fusion | flops 488546304 | bytes 4514816 | tf_op jit(solution)/shard_map/dot_general | solution.py:24
  65.8 0.0 copy-done.2
  65.9 0.0 copy-done.3
  65.9 2.4 %fusion.1 = (f32[256]{0:T(256)S(1)}, bf16[256,4224]{1,0:T(8,128)(2,1)}) fusion(bf16[256,4224]{1,0:T(8,128)(2,1)S(1)} %copy-done, f32[256]{0:T(256)S(1)} %copy-done.2, bf16[4224,224]{1,0:T(8,128)(2,1)S(1)} %copy-done.3, f32[256]{0:T(256)S(1)} %fusion.16, bf16[256,448]{0,1:T(8,128)(2,1)S(1)} %copy-done.1), kind=kOutput, calls=%fused_computation.3 | convolution fusion | flops 490364672 | bytes 6450176 | tf_op jit(solution)/shard_map/dot_general | solution.py:18
  68.3 86.5 %reduce-scatter.2.cloned.1.call-done = f32[528,224]{1,0:T(8,128)} async-done(((f32[4224,224]{1,0:T(8,128)}), f32[528,224]{1,0:T(8,128)}) %reduce-scatter.2.cloned.1.call-update) | async-done | bytes 473104 | tf_op jit(solution)/shard_map/reduce_scatter | solution.py:28
  154.8 0.0 all-reduce.2.cloned.1.call-update
  154.8 0.7 pad_maximum_fusion
  155.6 0.6 fusion.14
  156.1 34.1 %all-reduce.2.cloned.1.call-done = f32[528,224]{1,0:T(8,128)} async-done(((f32[528,224]{1,0:T(8,128)}), f32[528,224]{1,0:T(8,128)}) %all-reduce.2.cloned.1.call-update) | async-done | bytes 473104 | tf_op jit(solution)/shard_map/psum | solution.py:36
  190.2 1.9 copy.11
  (1 shorter events, 0.0 us)
Async XLA Ops:
  7.2 55.7 %all-gather.2.cloned.1.call-start = ((), (), s32[]{:S(2)}) async-start(), calls=%async_computation.1 | async-start | bytes 2433024 | tf_op jit(solution)/shard_map/all_gather | solution.py:17
  7.9 146.9 %reduce-scatter.2.cloned.1.call-start = ((), (), s32[]{:S(2)}) async-start(), calls=%async_computation.2 | async-start | bytes 4866048 | tf_op jit(solution)/shard_map/reduce_scatter | solution.py:28
  13.8 49.1 %copy-start = (bf16[256,4224]{1,0:T(8,128)(2,1)S(1)}, bf16[256,4224]{1,0:T(8,128)(2,1)}, u32[]{:S(2)}) copy-start(bf16[256,4224]{1,0:T(8,128)(2,1)} %param.9) | copy-start | bytes 6488068
  13.8 49.1 %copy-start.1 = (bf16[256,448]{0,1:T(8,128)(2,1)S(1)}, bf16[256,448]{0,1:T(8,128)(2,1)}, u32[]{:S(2)}) copy-start(bf16[256,448]{0,1:T(8,128)(2,1)} %param.5) | copy-start | bytes 688132
  13.8 52.0 %copy-start.2 = (f32[256]{0:T(256)S(1)}, f32[256]{0:T(256)}, u32[]{:S(2)}) copy-start(f32[256]{0:T(256)} %param.6) | copy-start | bytes 3076
  13.9 176.3 %all-reduce.2.cloned.1.call-start = ((), (), s32[]{:S(2)}) async-start(), calls=%async_computation.3 | async-start | bytes 1081344 | tf_op jit(solution)/shard_map/psum | solution.py:36
  62.9 3.0 %copy-start.3 = (bf16[4224,224]{1,0:T(8,128)(2,1)S(1)}, bf16[4224,224]{1,0:T(8,128)(2,1)}, u32[]{:S(2)}) copy-start(bf16[4224,224]{1,0:T(8,128)(2,1)} %all-gather.2.cloned.1.call-done) | copy-start | bytes 5677060
Sparse Core Ops, SparseCore 0:
  10.2 52.6 all-gather.1
  66.5 88.3 reduce-scatter.1
  157.3 32.8 all-reduce.1
where the time goes:
time: 199 us
  waiting for transfers between devices  170 us (85%)
  between operations  14.4 us (7%)
  matrix products  9.91 us (5%)
    reduce_scatter x1, waiting for transfers between devices, per_device(): lax.psum_scatter(lax.dot_general(grad_full, hidden, (((0,), (0,)), ((), (...  86.5 us
    all_gather x1, waiting for transfers between devices, per_device(): gathered = lax.all_gather(down_weight, 'shard', axis=0, tiled=True)  49 us
    psum x1, waiting for transfers between devices, per_device(): grad_down = lax.psum(owned, 'dp')  34.1 us
    dot_general x1, matrix products, per_device(): lax.dot_general(grad_full, hidden, (((0,), (0,)), ((), ())), preferred_el...  4.53 us
  transfers between devices with their start and end apart: 3, of which 3 were waited for; matrix products, arithmetic and copies ran while one was open for 6% of the time, Pallas kernels for 0%

commit v1 on v0

--- a/solution.py
+++ b/solution.py
@@ -1,10 +1,315 @@
+import functools
+
 import jax
 import jax.numpy as jnp
 from jax import lax
+from jax.experimental import pallas as pl
+from jax.experimental.pallas import tpu as pltpu
 from jax.sharding import PartitionSpec as P
 
-
-def per_device(gate_up, route_weight, live_rows, down_weight, out_grad):
+LANES = 128
+F32 = jnp.float32
+BF16 = jnp.bfloat16
+
+
+def kernel(
+    gate_up, route_weight, live_rows, weight, out_grad,
+    expert_out, grad_gate_up, grad_route, grad_down,
+    og, gf, eo, hid, wg, acc, psend, crecv,
+    xs0, xr0, ys0, yr0, xs1, xr1, ys1, yr1, zs, zr, fin,
+    og_sem, eo_sem, w_recv, w_send, r_recv, r_send, z_recv, f_recv,
+):
+    slots, features = og.shape
+    own_rows = weight.shape[0]
+    units = weight.shape[1]
+    region = 2 * own_rows
+    chunk = 3 * LANES
+    chunks = features // chunk
+    first_half = (2 * region + chunk - 1) // chunk
+
+    me_s, me_d = lax.axis_index("shard"), lax.axis_index("dp")
+    z, y, x, c = me_s // 2, me_s % 2, me_d // 2, me_d % 2
+    home = lax.rem(z, 2) == c
+
+    def device(zz, yy, xx, cc):
+        return (zz * 2 + yy, xx * 2 + cc)
+
+    to_x, to_y, to_c = device(z, y, 1 - x, c), device(z, 1 - y, x, c), device(z, y, x, 1 - c)
+    others_z = [lax.rem(z + d, 4) for d in (1, 2, 3)]
+
+    def rows(zz, yy):
+        return pl.ds(pl.multiple_of((zz * 2 + yy) * own_rows, 16), own_rows)
+
+    def plane(zz):
+        return pl.ds(pl.multiple_of(zz * region, 16), region)
+
+    def remote(src, dst, send, recv, dev):
+        return pltpu.make_async_remote_copy(
+            src_ref=src, dst_ref=dst, send_sem=send, recv_sem=recv,
+            device_id=dev, device_id_type=pl.DeviceIdType.MESH,
+        )
+
+    load = pltpu.make_async_copy(out_grad, og, og_sem)
+    load.start()
+    barrier = pltpu.get_barrier_semaphore()
+    partners = [to_x, to_y, to_c] + [device(zz, y, x, c) for zz in others_z]
+
+    wg[0, rows(z, y), :] = weight[:, :LANES]
+    wg[1, rows(z, y), :] = jnp.concatenate(
+        [weight[:, LANES:], jnp.zeros((own_rows, 2 * LANES - units), BF16)], axis=1
+    )
+    for dev in partners:
+        pl.semaphore_signal(barrier, inc=1, device_id=dev, device_id_type=pl.DeviceIdType.MESH)
+
+    live = (lax.broadcasted_iota(jnp.int32, (slots, LANES), 0) < live_rows[0]).astype(F32)
+    scale = jnp.broadcast_to(route_weight[...], (LANES, slots)).T
+    live_scale = live * scale
+
+    def gates():
+        both = gate_up[...].astype(F32)
+        gate, up = both[:, :units], both[:, units:]
+        sig = jax.nn.sigmoid(gate)
+        return gate, up, sig, gate * sig
+
+    _, up, _, activated = gates()
+    hidden = live[:, :1] * activated * up
+    hid[...] = jnp.concatenate(
+        [hidden, jnp.zeros((slots, 2 * LANES - units), F32)], axis=1
+    ).astype(BF16)
+    pl.semaphore_wait(barrier, len(partners))
+
+    pending = []
+    count = {"w": 0, "r": 0}
+
+    def begin(kind, src, dst, recv, dev, cond=None):
+        sems = w_send if kind == "w" else r_send
+        copy = remote(src, dst, sems.at[count[kind]], recv, dev)
+        count[kind] += 1
+        pending.append((copy, cond))
+        if cond is None:
+            copy.start()
+        else:
+            pl.when(cond)(copy.start)
+
+    def arrived(ref, recv, cond=None):
+        copy = remote(ref, ref, w_send.at[0], recv, to_x)
+        if cond is None:
+            copy.wait_recv()
+        else:
+            pl.when(cond)(copy.wait_recv)
+
+    def w_piece(zz, yy, t):
+        return wg.at[t, rows(zz, yy)], w_recv.at[t, zz * 2 + yy]
+
+    def w_give(zz, yy, t, dev, cond=None):
+        ref, sem = w_piece(zz, yy, t)
+        begin("w", ref, ref, sem, dev, cond)
+
+    def w_take(zz, yy, t, cond=None):
+        ref, sem = w_piece(zz, yy, t)
+        arrived(ref, sem, cond)
+
+    for zz in others_z:
+        w_give(z, y, x, device(zz, y, x, c), home)
+
+    load.wait()
+    wide = jnp.concatenate([live_scale] * 3, axis=1)
+
+    def partial(i, carry):
+        at = pl.ds(pl.multiple_of(i * chunk, LANES), chunk)
+        g = (wide * og[:, at].astype(F32)).astype(BF16)
+        gf[:, at] = g
+        p = lax.dot_general(g, hid[...], (((0,), (0,)), ((), ())), preferred_element_type=F32)
+        for t in (0, 1):
+            part = p[:, t * LANES:(t + 1) * LANES]
+            acc[t, at, :] = part
+            psend[t, at, :] = part.astype(BF16)
+        return carry
+
+    for k, (low, high) in enumerate(((0, first_half), (first_half, chunks))):
+        lax.fori_loop(low, high, partial, 0)
+        for t in (0, 1):
+            begin("r", psend.at[t, plane(1 - c + 2 * k)], crecv.at[t, k], r_recv.at[2 * k + t], to_c)
+
+    zk = [c, c + 2]
+    far = [zk[0] != z, zk[1] != z]
+
+    for t in (0, 1):
+        arrived(crecv.at[t, 0], r_recv.at[t])
+    xs0[...] = (acc[1 - x, plane(zk[0]), :] + crecv[1 - x, 0].astype(F32)).astype(BF16)
+    begin("r", xs0, xr0, r_recv.at[4], to_x)
+    acc[x, plane(zk[0]), :] += crecv[x, 0].astype(F32)
+    for t in (0, 1):
+        arrived(crecv.at[t, 1], r_recv.at[2 + t])
+
+    def half(yy):
+        return pl.ds(pl.multiple_of(yy * own_rows, 16), own_rows)
+
+    for t in (0, 1):
+        ys1[t] = (acc[t, rows(zk[1], 1 - y), :] + crecv[t, 1, half(1 - y), :].astype(F32)).astype(BF16)
+    begin("r", ys1, yr1, r_recv.at[5], to_y)
+    for t in (0, 1):
+        acc[t, rows(zk[1], y), :] += crecv[t, 1, half(y), :].astype(F32)
+
+    w_take(zk[0], y, x, far[0])
+    w_give(zk[0], y, x, to_y)
+    w_give(zk[0], y, x, to_x, far[0])
+    w_give(zk[0], y, x, to_c, far[0])
+    w_take(zk[1], y, x, far[1])
+    w_give(zk[1], y, x, to_x, far[1])
+    w_give(zk[1], y, x, to_y)
+    w_give(zk[1], y, x, to_c, far[1])
+
+    arrived(xr0, r_recv.at[4])
+    ys0[...] = (acc[x, rows(zk[0], 1 - y), :] + xr0[half(1 - y), :].astype(F32)).astype(BF16)
+    begin("r", ys0, yr0, r_recv.at[6], to_y)
+    acc[x, rows(zk[0], y), :] += xr0[half(y), :].astype(F32)
+    arrived(yr1, r_recv.at[5])
+    xs1[...] = (acc[1 - x, rows(zk[1], y), :] + yr1[1 - x].astype(F32)).astype(BF16)
+    begin("r", xs1, xr1, r_recv.at[7], to_x)
+    acc[x, rows(zk[1], y), :] += yr1[x].astype(F32)
+
+    w_take(zk[0], 1 - y, x)
+    w_give(zk[0], 1 - y, x, to_x)
+    w_give(zk[0], 1 - y, x, to_c)
+    w_take(zk[1], y, 1 - x, far[1])
+    w_give(zk[1], y, 1 - x, to_y)
+    w_give(zk[1], y, 1 - x, to_c, far[1])
+    w_take(zk[0], y, 1 - x, far[0])
+    w_give(zk[0], y, 1 - x, to_c, far[0])
+    w_take(zk[1], 1 - y, x)
+    w_give(zk[1], 1 - y, x, to_c)
+
+    for k, buf in ((0, yr0), (1, xr1)):
+        arrived(buf, r_recv.at[6 + k])
+        acc[x, rows(zk[k], y), :] += buf[...].astype(F32)
+        zs[k] = acc[x, rows(zk[k], y), :].astype(BF16)
+        begin("r", zs.at[k], zr.at[z], z_recv.at[z], device(zk[k], y, x, c), far[k])
+
+    w_take(zk[0], 1 - y, 1 - x)
+    w_give(zk[0], 1 - y, 1 - x, to_c)
+    w_take(zk[1], 1 - y, 1 - x)
+    w_give(zk[1], 1 - y, 1 - x, to_c)
+
+    away = jnp.logical_not(home)
+
+    @pl.when(home)
+    def _():
+        total = acc[x, rows(z, y), :]
+        for zz in others_z:
+            arrived(zr.at[zz], z_recv.at[zz])
+            total = total + zr[zz].astype(F32)
+        fin[x] = total
+
+    begin("r", fin.at[x], fin.at[x], f_recv.at[x], to_x, home)
+    begin("r", fin.at[x], fin.at[x], f_recv.at[x], to_c, home)
+
+    for k in (0, 1):
+        zz = 1 - c + 2 * k
+        for yy in (0, 1):
+            mine = jnp.logical_and(zz == z, yy == y)
+            for t in (0, 1):
+                w_take(zz, yy, t, jnp.logical_not(mine))
+
+    wide_route = jnp.concatenate([scale] * 3, axis=1)
+
+    def store(i):
+        at = pl.ds(pl.multiple_of(i * chunk, LANES), chunk)
+        return pltpu.make_async_copy(eo.at[:, at], expert_out.at[:, at], eo_sem.at[i])
+
+    def outputs(i, carry):
+        grad_hidden, route = carry
+        at = pl.ds(pl.multiple_of(i * chunk, LANES), chunk)
+        w = jnp.concatenate([wg[0, at, :], wg[1, at, :]], axis=1)
+        full = lax.dot_general(hid[...], w, (((1,), (1,)), ((), ())), preferred_element_type=F32)
+        eo[:, at] = (wide_route * full).astype(BF16)
+        prod = og[:, at].astype(F32) * full
+        route = route + prod[:, :LANES] + prod[:, LANES:2 * LANES] + prod[:, 2 * LANES:]
+        grad_hidden = grad_hidden + jnp.dot(gf[:, at], w, preferred_element_type=F32)
+        store(i).start()
+        return grad_hidden, route
+
+    grad_hidden, route = lax.fori_loop(
+        0, chunks, outputs,
+        (jnp.zeros((slots, 2 * LANES), F32), jnp.zeros((slots, LANES), F32)),
+    )
+    grad_route[...] = jnp.sum((live * route).T, axis=0, keepdims=True)
+    gate, up, sig, activated = gates()
+    grad_hidden = grad_hidden[:, :units]
+    grad_gate = grad_hidden * up * sig * (1.0 + gate * (1.0 - sig))
+    grad_gate_up[...] = jnp.concatenate([grad_gate, grad_hidden * activated], axis=1).astype(BF16)
+
+    arrived(fin.at[1 - x], f_recv.at[1 - x], home)
+    begin("r", fin.at[1 - x], fin.at[1 - x], f_recv.at[1 - x], to_c, home)
+    arrived(fin.at[x], f_recv.at[x], away)
+    arrived(fin.at[1 - x], f_recv.at[1 - x], away)
+    grad_down[:, :LANES] = fin[0]
+    grad_down[:, LANES:] = fin[1, :, :units - LANES]
+
+    for copy, cond in pending:
+        if cond is None:
+            copy.wait_send()
+        else:
+            pl.when(cond)(copy.wait_send)
+
+    def drain(i, carry):
+        store(i).wait()
+        return carry
+
+    lax.fori_loop(0, chunks, drain, 0)
+
+
+def fused(gate_up, route_weight, live_rows, down_weight, out_grad):
+    slots, features = out_grad.shape
+    own_rows, units = down_weight.shape
+    region = 2 * own_rows
+    chunks = features // (3 * LANES)
+    vmem = functools.partial(pl.BlockSpec, memory_space=pltpu.VMEM)
+    hbm = functools.partial(pl.BlockSpec, memory_space=pl.ANY)
+    dma = pltpu.SemaphoreType.DMA
+    expert_out, grad_gate_up, grad_route, grad_down = pl.pallas_call(
+        kernel,
+        out_shape=(
+            jax.ShapeDtypeStruct((slots, features), BF16),
+            jax.ShapeDtypeStruct(gate_up.shape, BF16),
+            jax.ShapeDtypeStruct((1, slots), F32),
+            jax.ShapeDtypeStruct((own_rows, units), F32),
+        ),
+        in_specs=[vmem(), vmem(), pl.BlockSpec(memory_space=pltpu.SMEM), vmem(), hbm()],
+        out_specs=(hbm(), vmem(), vmem(), vmem()),
+        scratch_shapes=[
+            pltpu.VMEM((slots, features), BF16),
+            pltpu.VMEM((slots, features), BF16),
+            pltpu.VMEM((slots, features), BF16),
+            pltpu.VMEM((slots, 2 * LANES), BF16),
+            pltpu.VMEM((2, features, LANES), BF16),
+            pltpu.VMEM((2, features, LANES), F32),
+            pltpu.VMEM((2, features, LANES), BF16),
+            pltpu.VMEM((2, 2, region, LANES), BF16),
+            pltpu.VMEM((region, LANES), BF16),
+            pltpu.VMEM((region, LANES), BF16),
+            pltpu.VMEM((own_rows, LANES), BF16),
+            pltpu.VMEM((own_rows, LANES), BF16),
+            pltpu.VMEM((own_rows, LANES), BF16),
+            pltpu.VMEM((own_rows, LANES), BF16),
+            pltpu.VMEM((2, own_rows, LANES), BF16),
+            pltpu.VMEM((2, own_rows, LANES), BF16),
+            pltpu.VMEM((2, own_rows, LANES), BF16),
+            pltpu.VMEM((4, own_rows, LANES), BF16),
+            pltpu.VMEM((2, own_rows, LANES), F32),
+            dma, dma((chunks,)), dma((2, 8)), dma((24,)), dma((8,)), dma((16,)), dma((4,)), dma((2,)),
+        ],
+        compiler_params=pltpu.CompilerParams(
+            collective_id=0, has_side_effects=True, vmem_limit_bytes=40 * 2**20
+        ),
+        cost_estimate=pl.CostEstimate(
+            flops=6 * slots * features * units, bytes_accessed=6 * slots * features, transcendentals=0
+        ),
+    )(gate_up, route_weight.reshape(1, slots), live_rows, down_weight, out_grad)
+    return expert_out, grad_gate_up, grad_route.reshape(slots), grad_down
+
+
+def plain(gate_up, route_weight, live_rows, down_weight, out_grad):
     slot_count = gate_up.shape[0]
     hidden_units = gate_up.shape[1] // 2
     row_mask = (lax.iota(jnp.int32, slot_count) < live_rows[0]).astype(jnp.float32)[:, None]
@@ -38,6 +343,7 @@
 
 
 def solution(mesh):
+    shape = (mesh.shape["shard"], mesh.shape["dp"])
     in_specs = (
         P(("shard", "dp"), None),
         P(("shard", "dp")),
@@ -52,5 +358,6 @@
         P("shard", None),
     )
     return jax.shard_map(
-        per_device, mesh=mesh, in_specs=in_specs, out_specs=out_specs, check_vma=False
-    )
+        fused if shape == (8, 4) else plain,
+        mesh=mesh, in_specs=in_specs, out_specs=out_specs, check_vma=False,
+    )

time: 199 us -> 51.6 us (0.26)
  waiting for transfers between devices: 170 us -> 0 us
  Pallas kernels: 0 us -> 42.2 us
  between operations: 14.4 us -> 1.3 us
  matrix products: 9.91 us -> 0 us
  local copies, waits for them, and re-layouts: 1.9 us -> 7.84 us
    reduce_scatter x1 -> x0, waiting for transfers between devices: 86.5 us -> none  [per_device(): lax.psum_scatter(lax.dot_general(grad_full, hidden, (((0,), (0,)), ((), (...]
    all_gather x1 -> x0, waiting for transfers between devices: 49 us -> none  [per_device(): gathered = lax.all_gather(down_weight, 'shard', axis=0, tiled=True)]
    pallas_call x0 -> x1, Pallas kernels: none -> 42.2 us  [fused(): pl.pallas_call(kernel, out_shape=(jax.ShapeDtypeStruct((slots, features),...]
    psum x1 -> x0, waiting for transfers between devices: 34.1 us -> none  [per_device(): grad_down = lax.psum(owned, 'dp')]
    dot_general x3 -> x0, matrix products: 9.91 us -> none  [the longest x1 4.53 us: per_device(): lax.dot_general(grad_full, hidden, (((0,), (0,)), ((), ())), preferred_el...]
    unnamed x9 -> x11, local copies, waits for them, and re-layouts: 1.9 us -> 7.84 us
  transfers between devices with their start and end apart: 3 -> 0, of which waited for: 3 -> 0; matrix products, arithmetic and copies ran while one was open for 6% -> 0% of each run, Pallas kernels for 0% -> 0%
where the time goes in v1:
time: 51.6 us; the launch traced here: 51.3 us
  Pallas kernels  42.2 us (82%)
  local copies, waits for them, and re-layouts  7.84 us (15%)
  between operations  1.3 us (3%)
    pallas_call x1, Pallas kernels, fused(): pl.pallas_call(kernel, out_shape=(jax.ShapeDtypeStruct((slots, features),...  42.2 us
    unnamed x11, local copies, waits for them, and re-layouts  7.84 us

profile of v1, /device:TPU:0, one launch (start us, length us, event | category | flops | bytes accessed | tf_op | source)
XLA Modules:
  0.0 51.3 jit_solution(9357001288755261937)
XLA Ops:
  1.3 1.1 %copy.9.gate_up = bf16[256,448]{1,0:T(8,128)(2,1)S(1)} copy(bf16[256,448]{0,1:T(8,128)(2,1)} %param.5) | data formatting | bytes 458752 | tf_op args[0]
  2.4 0.0 copy-start
  2.4 1.6 %copy-done = bf16[256,4224]{1,0:T(8,128)(2,1)S(1)} copy-done((bf16[256,4224]{1,0:T(8,128)(2,1)S(1)}, bf16[256,4224]{1,0:T(8,128)(2,1)}, u32[]{:S(2)}) %copy-start) | copy-done | bytes 2162712
  4.0 0.0 copy-start.1
  4.0 1.0 %copy-done.1 = bf16[528,224]{1,0:T(8,128)(2,1)S(1)} copy-done((bf16[528,224]{1,0:T(8,128)(2,1)S(1)}, bf16[528,224]{1,0:T(8,128)(2,1)}, u32[]{:S(2)}) %copy-start.1) | copy-done | bytes 236568
  4.9 0.0 copy-start.2
  4.9 0.7 %copy-done.2 = f32[256]{0:T(256)S(1)} copy-done((f32[256]{0:T(256)S(1)}, f32[256]{0:T(256)}, u32[]{:S(2)}) %copy-start.2) | copy-done | bytes 1048
  5.6 42.2 %shard_map.84 = (bf16[256,4224]{1,0:T(8,128)(2,1)S(1)}, bf16[256,448]{1,0:T(8,128)(2,1)S(1)}, f32[1,256]{1,0:T(1,128)S(1)}, f32[528,224]{1,0:T(8,128)S(1)}) custom-call(bf16[256,448]{1,0:T(8,128)(2,1)S(1)} %copy.9.gate_up, f32[1,256]{1,0:T(1,128)S(1)} %bitcast.3, s32[1]{0:T(128)S(6)} %copy.14.live_rows, bf16[528,224]{1,0:T(8,128)(2,1)S(1)} %copy-done.1, ...), custom_call_target="tpu_custom_call" | custom-call | flops 1453326336 | bytes 6488064 | tf_op jit(solution)/shard_map/pallas_call | solution.py:270
  47.8 0.8 %copy.10 = bf16[256,448]{0,1:T(8,128)(2,1)} copy(bf16[256,448]{1,0:T(8,128)(2,1)S(1)} %get-tuple-element.13) | data formatting | bytes 458752
  48.6 1.3 %copy.15 = bf16[256,4224]{1,0:T(8,128)(2,1)} copy(bf16[256,4224]{1,0:T(8,128)(2,1)S(1)} %get-tuple-element.20) | data formatting | bytes 4325376
  49.9 0.6 %copy.16 = f32[256]{0:T(256)} copy(f32[256]{0:T(256)S(1)} %bitcast.2) | data formatting | bytes 2048
  50.5 0.8 %copy.17 = f32[528,224]{1,0:T(8,128)} copy(f32[528,224]{1,0:T(8,128)S(1)} %get-tuple-element.23) | data formatting | bytes 946176
Async XLA Ops:
  2.4 1.6 %copy-start = (bf16[256,4224]{1,0:T(8,128)(2,1)S(1)}, bf16[256,4224]{1,0:T(8,128)(2,1)}, u32[]{:S(2)}) copy-start(bf16[256,4224]{1,0:T(8,128)(2,1)} %out_grad.1) | copy-start | bytes 6488068
  4.0 1.0 %copy-start.1 = (bf16[528,224]{1,0:T(8,128)(2,1)S(1)}, bf16[528,224]{1,0:T(8,128)(2,1)}, u32[]{:S(2)}) copy-start(bf16[528,224]{1,0:T(8,128)(2,1)} %weight.1) | copy-start | bytes 709636
  4.9 0.7 %copy-start.2 = (f32[256]{0:T(256)S(1)}, f32[256]{0:T(256)}, u32[]{:S(2)}) copy-start(f32[256]{0:T(256)} %param.6) | copy-start | bytes 3076

commit v2 on v1

v2 whole, which is shorter than its diff:
```python
import jax
import jax.numpy as jnp
from jax import lax
from jax.experimental import pallas as pl
from jax.experimental.pallas import tpu as pltpu
from jax.sharding import PartitionSpec as P

LANES = 128
F32 = jnp.float32
BF16 = jnp.bfloat16


def kernel(
    gate_up, route_weight, live_rows, weight, out_grad,
    eo, grad_gate_up, grad_route, grad_down,
    og, gu, rw, wt, gf, hid, wg, acc, psend, crecv,
    xs0, xr0, ys0, yr0, xs1, xr1, ys1, yr1, zs, zr, tot, fin,
    in_sem, w_recv, w_send, c_recv, r_recv, h_recv, r_send, z_recv, f_recv,
):
    slots, features = og.shape
    own_rows = wt.shape[0]
    units = wt.shape[1]
    region = 2 * own_rows
    chunk = 3 * LANES
    chunks = features // chunk
    first_half = (2 * region + chunk - 1) // chunk
    split = (own_rows // 2 + 15) // 16 * 16
    halves = [pl.ds(0, split), pl.ds(split, own_rows - split)]

    loads = [
        pltpu.make_async_copy(src, dst, in_sem.at[i])
        for i, (src, dst) in enumerate(
            ((weight, wt), (gate_up, gu), (route_weight, rw), (out_grad, og))
        )
    ]
    for copy in loads:
        copy.start()

    me_s, me_d = lax.axis_index("shard"), lax.axis_index("dp")
    z, y, x, c = me_s // 2, me_s % 2, me_d // 2, me_d % 2
    home = lax.rem(z, 2) == c
    away = jnp.logical_not(home)

    def device(zz, yy, xx, cc):
        return (zz * 2 + yy, xx * 2 + cc)

    to_x, to_y, to_c = device(z, y, 1 - x, c), device(z, 1 - y, x, c), device(z, y, x, 1 - c)
    others_z = [lax.rem(z + d, 4) for d in (1, 2, 3)]

    barrier = pltpu.get_barrier_semaphore()
    partners = [to_x, to_y, to_c] + [device(zz, y, x, c) for zz in others_z]
    for dev in partners:
        pl.semaphore_signal(barrier, inc=1, device_id=dev, device_id_type=pl.DeviceIdType.MESH)

    def rows(zz, yy):
        return pl.ds(pl.multiple_of((zz * 2 + yy) * own_rows, 16), own_rows)

    def rows_of(zz, yy, part):
        return pl.ds(pl.multiple_of((zz * 2 + yy) * own_rows + part.start, 16), part.size)

    def plane(zz):
        return pl.ds(pl.multiple_of(zz * region, 16), region)

    pending = []
    count = {"w": 0, "r": 0}

    def begin(kind, src, dst, recv, dev, cond=None):
        sems = w_send if kind == "w" else r_send
        copy = pltpu.make_async_remote_copy(
            src_ref=src, dst_ref=dst, send_sem=sems.at[count[kind]], recv_sem=recv,
            device_id=dev, device_id_type=pl.DeviceIdType.MESH,
        )
        count[kind] += 1
        pending.append((copy, cond))
        if cond is None:
            copy.start()
        else:
            pl.when(cond)(copy.start)

    def arrived(ref, recv, cond=None):
        copy = pltpu.make_async_remote_copy(
            src_ref=ref, dst_ref=ref, send_sem=w_send.at[0], recv_sem=recv,
            device_id=to_x, device_id_type=pl.DeviceIdType.MESH,
        )
        if cond is None:
            copy.wait_recv()
        else:
            pl.when(cond)(copy.wait_recv)

    def w_piece(zz, yy, t):
        return wg.at[t, rows(zz, yy)], w_recv.at[t, zz * 2 + yy]

    def w_give(zz, yy, t, dev, cond=None):
        ref, sem = w_piece(zz, yy, t)
        begin("w", ref, ref, sem, dev, cond)

    def w_take(zz, yy, t, cond=None):
        ref, sem = w_piece(zz, yy, t)
        arrived(ref, sem, cond)

    loads[0].wait()
    wg[0, rows(z, y), :] = wt[:, :LANES]
    wg[1, rows(z, y), :] = jnp.concatenate(
        [wt[:, LANES:], jnp.zeros((own_rows, 2 * LANES - units), BF16)], axis=1
    )
    pl.semaphore_wait(barrier, len(partners))

    zk = [c, c + 2]
    far = [zk[0] != z, zk[1] != z]
    near = [zk[0] == z, zk[1] == z]

    for zz in others_z:
        w_give(z, y, x, device(zz, y, x, c), home)
    w_give(z, y, x, to_y, home)

    loads[1].wait()
    loads[2].wait()

    def gates():
        gate, up = gu[:units, :].astype(F32), gu[units:, :].astype(F32)
        sig = jax.nn.sigmoid(gate)
        return gate, up, sig, gate * sig

    _, up, _, activated = gates()
    live_row = (lax.broadcasted_iota(jnp.int32, (1, slots), 1) < live_rows[0]).astype(F32)
    hidden = live_row * activated * up
    hid[...] = jnp.concatenate(
        [hidden, jnp.zeros((2 * LANES - units, slots), F32)], axis=0
    ).T.astype(BF16)
    live = (lax.broadcasted_iota(jnp.int32, (slots, LANES), 0) < live_rows[0]).astype(F32)
    scale = jnp.broadcast_to(rw[...], (LANES, slots)).T
    wide = jnp.concatenate([live * scale] * 3, axis=1)
    loads[3].wait()

    def partial(i, carry):
        at = pl.ds(pl.multiple_of(i * chunk, LANES), chunk)
        g = (wide * og[:, at].astype(F32)).astype(BF16)
        gf[:, at] = g
        p = lax.dot_general(g, hid[...], (((0,), (0,)), ((), ())), preferred_element_type=F32)
        for t in (0, 1):
            part = p[:, t * LANES:(t + 1) * LANES]
            acc[t, at, :] = part
            psend[t, at, :] = part.astype(BF16)
        return carry

    for k, (low, high) in enumerate(((0, first_half), (first_half, chunks))):
        lax.fori_loop(low, high, partial, 0)
        for t in (0, 1):
            begin("r", psend.at[t, plane(1 - c + 2 * k)], crecv.at[t, k], c_recv.at[k, t], to_c)

    def pair(t, k, yy, part=None):
        part = pl.ds(0, own_rows) if part is None else part
        there = pl.ds(pl.multiple_of(yy * own_rows + part.start, 16), part.size)
        return acc[t, rows_of(zk[k], yy, part), :] + crecv[t, k, there, :].astype(F32)

    for t in (0, 1):
        arrived(crecv.at[t, 0], c_recv.at[0, t])
    for i, yy in enumerate((1 - y, y)):
        xs0[i] = pair(1 - x, 0, yy).astype(BF16)
        begin("r", xs0.at[i], xr0.at[i], r_recv.at[0, i], to_x)
    for t in (0, 1):
        arrived(crecv.at[t, 1], c_recv.at[1, t])
    for i, t in enumerate((1 - x, x)):
        ys1[i] = pair(t, 1, 1 - y).astype(BF16)
        begin("r", ys1.at[i], yr1.at[i], r_recv.at[1, i], to_y)

    w_take(zk[0], y, x, far[0])
    w_give(zk[0], y, x, to_y, far[0])
    w_give(zk[0], y, x, to_x, far[0])
    w_give(zk[0], y, x, to_c, far[0])
    w_take(zk[1], y, x, far[1])
    w_give(zk[1], y, x, to_x, far[1])
    w_give(zk[1], y, x, to_y, far[1])
    w_give(zk[1], y, x, to_c, far[1])

    arrived(xr0.at[0], r_recv.at[0, 0])
    for h, part in enumerate(halves):
        ys0[part, :] = (pair(x, 0, 1 - y, part) + xr0[0, part, :].astype(F32)).astype(BF16)
        begin("r", ys0.at[part], yr0.at[part], h_recv.at[0, h], to_y)
    arrived(yr1.at[0], r_recv.at[1, 0])
    for h, part in enumerate(halves):
        xs1[part, :] = (pair(1 - x, 1, y, part) + yr1[0, part, :].astype(F32)).astype(BF16)
        begin("r", xs1.at[part], xr1.at[part], h_recv.at[1, h], to_x)

    w_take(zk[0], 1 - y, x)
    w_give(zk[0], 1 - y, x, to_x)
    w_give(zk[0], 1 - y, x, to_c)
    w_take(zk[1], y, 1 - x, far[1])
    w_give(zk[1], y, 1 - x, to_y)
    w_give(zk[1], y, 1 - x, to_c, far[1])
    w_take(zk[0], y, 1 - x, far[0])
    w_give(zk[0], y, 1 - x, to_c, far[0])
    w_take(zk[1], 1 - y, x)
    w_give(zk[1], 1 - y, x, to_c)

    arrived(xr0.at[1], r_recv.at[0, 1])
    arrived(yr1.at[1], r_recv.at[1, 1])
    for h, part in enumerate(halves):
        for k, (first, second) in enumerate(((xr0, yr0), (yr1, xr1))):
            arrived(second.at[part], h_recv.at[k, h])
            total = (
                pair(x, k, y, part) + first[1, part, :].astype(F32) + second[part, :].astype(F32)
            )
            zs[k, part, :] = total.astype(BF16)
            begin("r", zs.at[k, part], zr.at[z, part], z_recv.at[h, z], device(zk[k], y, x, c), far[k])

            @pl.when(near[k])
            def _():
                tot[part, :] = total

    w_take(zk[0], 1 - y, 1 - x)
    w_give(zk[0], 1 - y, 1 - x, to_c)
    w_take(zk[1], 1 - y, 1 - x)
    w_give(zk[1], 1 - y, 1 - x, to_c)
    for k in (0, 1):
        zz = 1 - c + 2 * k
        for yy in (0, 1):
            mine = jnp.logical_and(zz == z, yy == y)
            for t in (0, 1):
                w_take(zz, yy, t, jnp.logical_not(mine))

    wide_route = jnp.concatenate([scale] * 3, axis=1)

    def outputs(i, carry):
        grad_hidden, route = carry
        at = pl.ds(pl.multiple_of(i * chunk, LANES), chunk)
        w = jnp.concatenate([wg[0, at, :], wg[1, at, :]], axis=1)
        full = lax.dot_general(hid[...], w, (((1,), (1,)), ((), ())), preferred_element_type=F32)
        eo[:, at] = (wide_route * full).astype(BF16)
        prod = og[:, at].astype(F32) * full
        route = route + prod[:, :LANES] + prod[:, LANES:2 * LANES] + prod[:, 2 * LANES:]
        grad_hidden = grad_hidden + jnp.dot(gf[:, at], w, preferred_element_type=F32)
        return grad_hidden, route

    grad_hidden, route = lax.fori_loop(
        0, chunks, outputs,
        (jnp.zeros((slots, 2 * LANES), F32), jnp.zeros((slots, LANES), F32)),
    )
    grad_route[...] = jnp.sum((live * route).T, axis=0, keepdims=True)
    gate, up, sig, activated = gates()
    grad_hidden = grad_hidden.T[:units, :]
    grad_gate_up[:units, :] = (grad_hidden * up * sig * (1.0 + gate * (1.0 - sig))).astype(BF16)
    grad_gate_up[units:, :] = (grad_hidden * activated).astype(BF16)

    for h, part in enumerate(halves):
        @pl.when(home)
        def _():
            total = tot[part, :]
            for zz in others_z:
                arrived(zr.at[zz, part], z_recv.at[h, zz])
                total = total + zr[zz, part, :].astype(F32)
            fin[x, part, :] = total

        begin("r", fin.at[x, part], fin.at[x, part], f_recv.at[h, x], to_x, home)
        begin("r", fin.at[x, part], fin.at[x, part], f_recv.at[h, x], to_c, home)
    for h, part in enumerate(halves):
        arrived(fin.at[1 - x, part], f_recv.at[h, 1 - x], home)
        begin("r", fin.at[1 - x, part], fin.at[1 - x, part], f_recv.at[h, 1 - x], to_c, home)
    for h, part in enumerate(halves):
        arrived(fin.at[x, part], f_recv.at[h, x], away)
        arrived(fin.at[1 - x, part], f_recv.at[h, 1 - x], away)
    grad_down[:, :LANES] = fin[0]
    grad_down[:, LANES:] = fin[1, :, :units - LANES]

    for copy, cond in pending:
        if cond is None:
            copy.wait_send()
        else:
            pl.when(cond)(copy.wait_send)


def place(*refs):
    count = (len(refs) - 1) // 2
    copies = [
        pltpu.make_async_copy(refs[i], refs[count + i], refs[-1].at[i]) for i in range(count)
    ]
    for copy in copies:
        copy.start()
    for copy in copies:
        copy.wait()


def fused(gate_up, route_weight, live_rows, down_weight, out_grad):
    slots, features = out_grad.shape
    own_rows, units = down_weight.shape
    region = 2 * own_rows
    vmem = pl.BlockSpec(memory_space=pltpu.VMEM)
    hbm = pl.BlockSpec(memory_space=pltpu.HBM)
    dma = pltpu.SemaphoreType.DMA
    piece = (own_rows, LANES)
    shapes = (
        jax.ShapeDtypeStruct((slots, features), BF16),
        jax.ShapeDtypeStruct((2 * units, slots), BF16),
        jax.ShapeDtypeStruct((1, slots), F32),
        jax.ShapeDtypeStruct((own_rows, units), F32),
    )
    results = pl.pallas_call(
        kernel,
        out_shape=tuple(pltpu.VMEM(a.shape, a.dtype) for a in shapes),
        in_specs=[hbm, hbm, pl.BlockSpec(memory_space=pltpu.SMEM), hbm, hbm],
        out_specs=(vmem,) * 4,
        scratch_shapes=[
            pltpu.VMEM((slots, features), BF16),
            pltpu.VMEM((2 * units, slots), BF16),
            pltpu.VMEM((1, slots), F32),
            pltpu.VMEM((own_rows, units), BF16),
            pltpu.VMEM((slots, features), BF16),
            pltpu.VMEM((slots, 2 * LANES), BF16),
            pltpu.VMEM((2, features, LANES), BF16),
            pltpu.VMEM((2, features, LANES), F32),
            pltpu.VMEM((2, features, LANES), BF16),
            pltpu.VMEM((2, 2, region, LANES), BF16),
            pltpu.VMEM((2,) + piece, BF16),
            pltpu.VMEM((2,) + piece, BF16),
            pltpu.VMEM(piece, BF16),
            pltpu.VMEM(piece, BF16),
            pltpu.VMEM(piece, BF16),
            pltpu.VMEM(piece, BF16),
            pltpu.VMEM((2,) + piece, BF16),
            pltpu.VMEM((2,) + piece, BF16),
            pltpu.VMEM((2,) + piece, BF16),
            pltpu.VMEM((4,) + piece, BF16),
            pltpu.VMEM(piece, F32),
            pltpu.VMEM((2,) + piece, F32),
            dma((4,)), dma((2, 8)), dma((24,)), dma((2, 2)), dma((2, 2)), dma((2, 2)),
            dma((24,)), dma((2, 4)), dma((2, 2)),
        ],
        compiler_params=pltpu.CompilerParams(
            collective_id=0, has_side_effects=True, vmem_limit_bytes=58 * 2**20
        ),
        cost_estimate=pl.CostEstimate(
            flops=6 * slots * features * units, bytes_accessed=6 * slots * features, transcendentals=0
        ),
    )(gate_up.T, route_weight.reshape(1, slots), live_rows, down_weight, out_grad)
    expert_out, grad_gate_up, grad_route, grad_down = pl.pallas_call(
        place,
        out_shape=shapes,
        in_specs=[pl.BlockSpec(memory_space=pl.ANY)] * 4,
        out_specs=(hbm,) * 4,
        scratch_shapes=[dma((4,))],
        compiler_params=pltpu.CompilerParams(vmem_limit_bytes=2**20),
    )(*results)
    return expert_out, grad_gate_up.T, grad_route.reshape(slots), grad_down


def plain(gate_up, route_weight, live_rows, down_weight, out_grad):
    slot_count = gate_up.shape[0]
    hidden_units = gate_up.shape[1] // 2
    row_mask = (lax.iota(jnp.int32, slot_count) < live_rows[0]).astype(jnp.float32)[:, None]
    gate_pre = gate_up[:, :hidden_units].astype(jnp.float32)
    up_proj = gate_up[:, hidden_units:].astype(jnp.float32)
    sigmoid_gate = jax.nn.sigmoid(gate_pre)
    activated = gate_pre * sigmoid_gate
    hidden = (row_mask * activated * up_proj).astype(jnp.bfloat16)
    row_scale = route_weight[:, None]
    gathered = lax.all_gather(down_weight, "shard", axis=0, tiled=True)
    full = lax.dot_general(
        hidden, gathered, (((1,), (1,)), ((), ())), preferred_element_type=jnp.float32
    )
    expert_out = (row_scale * full).astype(jnp.bfloat16)
    grad_route = row_mask[:, 0] * jnp.sum(out_grad.astype(jnp.float32) * full, axis=1)
    grad_full = (row_mask * row_scale * out_grad.astype(jnp.float32)).astype(jnp.bfloat16)
    grad_hidden = jnp.dot(grad_full, gathered, preferred_element_type=jnp.float32)
    grad_gate = grad_hidden * up_proj * sigmoid_gate * (1.0 + gate_pre * (1.0 - sigmoid_gate))
    grad_up = grad_hidden * activated
    grad_gate_up = jnp.concatenate([grad_gate, grad_up], axis=1).astype(jnp.bfloat16)
    owned = lax.psum_scatter(
        lax.dot_general(
            grad_full, hidden, (((0,), (0,)), ((), ())), preferred_element_type=jnp.float32
        ),
        "shard",
        scatter_dimension=0,
        tiled=True,
    )
    grad_down = lax.psum(owned, "dp")
    return (expert_out, grad_gate_up, grad_route, grad_down)


def solution(mesh):
    shape = (mesh.shape["shard"], mesh.shape["dp"])
    in_specs = (
        P(("shard", "dp"), None),
        P(("shard", "dp")),
        P(("shard", "dp")),
        P("shard", None),
        P(("shard", "dp"), None),
    )
    out_specs = (
        P(("shard", "dp"), None),
        P(("shard", "dp"), None),
        P(("shard", "dp")),
        P("shard", None),
    )
    return jax.shard_map(
        fused if shape == (8, 4) else plain,
        mesh=mesh, in_specs=in_specs, out_specs=out_specs, check_vma=False,
    )
```

time: 51.6 us -> 44 us (0.85)
  local copies, waits for them, and re-layouts: 7.84 us -> 0 us
    unnamed x11 -> x0, local copies, waits for them, and re-layouts: 7.84 us -> none
    pallas_call x1 -> x2, Pallas kernels: 42.2 us -> 42.6 us  [the longest x1 41 us: fused(): pl.pallas_call(kernel, out_shape=tuple((pltpu.VMEM(a.shape, a.dtype) for...]
where the time goes in v2:
time: 44 us; the launch traced here: 43.9 us
  Pallas kernels  42.6 us (97%)
  between operations  1.29 us (3%)
    pallas_call x1, Pallas kernels, fused(): pl.pallas_call(kernel, out_shape=tuple((pltpu.VMEM(a.shape, a.dtype) for...  41 us
    pallas_call x1, Pallas kernels, fused(): pl.pallas_call(place, out_shape=shapes, in_specs=[pl.BlockSpec(memory_spa...  1.63 us

profile of v2, /device:TPU:0, one launch (start us, length us, event | category | flops | bytes accessed | tf_op | source)
XLA Modules:
  0.0 43.9 jit_solution(17058978898980510805)
XLA Ops:
  1.3 41.0 %shard_map.84 = (bf16[256,4224]{1,0:T(8,128)(2,1)S(1)}, bf16[448,256]{1,0:T(8,128)(2,1)S(1)}, f32[1,256]{1,0:T(1,128)S(1)}, f32[528,224]{1,0:T(8,128)S(1)}) custom-call(bf16[448,256]{1,0:T(8,128)(2,1)} %bitcast.4, f32[1,256]{1,0:T(1,128)} %bitcast.6, s32[1]{0:T(128)S(6)} %copy.9.live_rows, bf16[528,224]{1,0:T(8,128)(2,1)} %weight.1, bf16[256,4224]{1,0:T(8,128)(2,1)} %out_grad.1), custom_call_target="tpu_custom_call" | custom-call | flops 1453326336 | bytes 6488064 | tf_op jit(solution)/shard_map/pallas_call | solution.py:297
  42.2 1.6 %shard_map.85 = (bf16[256,4224]{1,0:T(8,128)(2,1)}, bf16[448,256]{1,0:T(8,128)(2,1)}, f32[1,256]{1,0:T(1,128)}, f32[528,224]{1,0:T(8,128)}) custom-call(bf16[256,4224]{1,0:T(8,128)(2,1)S(1)} %get-tuple-element.12.refs_0_, bf16[448,256]{1,0:T(8,128)(2,1)S(1)} %get-tuple-element.13.refs_1_, f32[1,256]{1,0:T(1,128)S(1)} %get-tuple-element.14.refs_2_, ...), custom_call_target="tpu_custom_call" | custom-call | tf_op jit(solution)/shard_map/pallas_call | solution.py:335

commit v3 on v2

--- a/solution.py
+++ b/solution.py
@@ -6,6 +6,7 @@
 from jax.sharding import PartitionSpec as P
 
 LANES = 128
+SLICES = 3
 F32 = jnp.float32
 BF16 = jnp.bfloat16
 
@@ -23,9 +24,8 @@
     region = 2 * own_rows
     chunk = 3 * LANES
     chunks = features // chunk
-    first_half = (2 * region + chunk - 1) // chunk
-    split = (own_rows // 2 + 15) // 16 * 16
-    halves = [pl.ds(0, split), pl.ds(split, own_rows - split)]
+    size = own_rows // SLICES
+    slices = [pl.ds(i * size, size) for i in range(SLICES)]
 
     loads = [
         pltpu.make_async_copy(src, dst, in_sem.at[i])
@@ -38,7 +38,7 @@
 
     me_s, me_d = lax.axis_index("shard"), lax.axis_index("dp")
     z, y, x, c = me_s // 2, me_s % 2, me_d // 2, me_d % 2
-    home = lax.rem(z, 2) == c
+    home = lax.rem(z, 2) == x
     away = jnp.logical_not(home)
 
     def device(zz, yy, xx, cc):
@@ -57,9 +57,6 @@
 
     def rows_of(zz, yy, part):
         return pl.ds(pl.multiple_of((zz * 2 + yy) * own_rows + part.start, 16), part.size)
-
-    def plane(zz):
-        return pl.ds(pl.multiple_of(zz * region, 16), region)
 
     pending = []
     count = {"w": 0, "r": 0}
@@ -87,15 +84,15 @@
         else:
             pl.when(cond)(copy.wait_recv)
 
-    def w_piece(zz, yy, t):
-        return wg.at[t, rows(zz, yy)], w_recv.at[t, zz * 2 + yy]
-
-    def w_give(zz, yy, t, dev, cond=None):
-        ref, sem = w_piece(zz, yy, t)
+    def w_piece(zz, yy, t, q):
+        return wg.at[t, rows_of(zz, yy, slices[q])], w_recv.at[t, zz * 2 + yy, q]
+
+    def w_give(zz, yy, t, q, dev, cond=None):
+        ref, sem = w_piece(zz, yy, t, q)
         begin("w", ref, ref, sem, dev, cond)
 
-    def w_take(zz, yy, t, cond=None):
-        ref, sem = w_piece(zz, yy, t)
+    def w_take(zz, yy, t, q, cond=None):
+        ref, sem = w_piece(zz, yy, t, q)
         arrived(ref, sem, cond)
 
     loads[0].wait()
@@ -103,16 +100,6 @@
     wg[1, rows(z, y), :] = jnp.concatenate(
         [wt[:, LANES:], jnp.zeros((own_rows, 2 * LANES - units), BF16)], axis=1
     )
-    pl.semaphore_wait(barrier, len(partners))
-
-    zk = [c, c + 2]
-    far = [zk[0] != z, zk[1] != z]
-    near = [zk[0] == z, zk[1] == z]
-
-    for zz in others_z:
-        w_give(z, y, x, device(zz, y, x, c), home)
-    w_give(z, y, x, to_y, home)
-
     loads[1].wait()
     loads[2].wait()
 
@@ -143,81 +130,135 @@
             psend[t, at, :] = part.astype(BF16)
         return carry
 
-    for k, (low, high) in enumerate(((0, first_half), (first_half, chunks))):
-        lax.fori_loop(low, high, partial, 0)
-        for t in (0, 1):
-            begin("r", psend.at[t, plane(1 - c + 2 * k)], crecv.at[t, k], c_recv.at[k, t], to_c)
-
-    def pair(t, k, yy, part=None):
-        part = pl.ds(0, own_rows) if part is None else part
-        there = pl.ds(pl.multiple_of(yy * own_rows + part.start, 16), part.size)
-        return acc[t, rows_of(zk[k], yy, part), :] + crecv[t, k, there, :].astype(F32)
-
-    for t in (0, 1):
-        arrived(crecv.at[t, 0], c_recv.at[0, t])
-    for i, yy in enumerate((1 - y, y)):
-        xs0[i] = pair(1 - x, 0, yy).astype(BF16)
-        begin("r", xs0.at[i], xr0.at[i], r_recv.at[0, i], to_x)
-    for t in (0, 1):
-        arrived(crecv.at[t, 1], c_recv.at[1, t])
-    for i, t in enumerate((1 - x, x)):
-        ys1[i] = pair(t, 1, 1 - y).astype(BF16)
-        begin("r", ys1.at[i], yr1.at[i], r_recv.at[1, i], to_y)
-
-    w_take(zk[0], y, x, far[0])
-    w_give(zk[0], y, x, to_y, far[0])
-    w_give(zk[0], y, x, to_x, far[0])
-    w_give(zk[0], y, x, to_c, far[0])
-    w_take(zk[1], y, x, far[1])
-    w_give(zk[1], y, x, to_x, far[1])
-    w_give(zk[1], y, x, to_y, far[1])
-    w_give(zk[1], y, x, to_c, far[1])
-
-    arrived(xr0.at[0], r_recv.at[0, 0])
-    for h, part in enumerate(halves):
+    lax.fori_loop(0, chunks, partial, 0)
+    pl.semaphore_wait(barrier, len(partners))
+
+    zk = [x, x + 2]
+    far = [zk[0] != z, zk[1] != z]
+    near = [zk[0] == z, zk[1] == z]
+    across = [lax.rem(z + 2, 4), 3 - z, z + 1 - 2 * lax.rem(z, 2)]
+
+    for k in (0, 1):
+        part = pl.ds(2 * k * region, 2 * region)
+        begin("r", psend.at[1 - c, part], crecv.at[part], c_recv.at[k], to_c)
+
+    for q in range(SLICES):
+        for zz in across:
+            w_give(z, y, c, q, device(zz, y, x, c), home)
+
+    def pair(u, k, yy, part):
+        at = rows_of(u + 2 * k, yy, part)
+        return acc[c, at, :] + crecv[at, :].astype(F32)
+
+    def sum_first(q):
+        part = slices[q]
+        for i in (0, 1):
+            yy, t = ((1 - y, 1 - x), (y, x))[i]
+            xs0[i, part, :] = pair(1 - x, 0, yy, part).astype(BF16)
+            begin("r", xs0.at[i, part], xr0.at[i, part], r_recv.at[0, i, q], to_x)
+            ys1[i, part, :] = pair(t, 1, 1 - y, part).astype(BF16)
+            begin("r", ys1.at[i, part], yr1.at[i, part], r_recv.at[1, i, q], to_y)
+
+    def sum_second(q):
+        part = slices[q]
+        arrived(xr0.at[0, part], r_recv.at[0, 0, q])
         ys0[part, :] = (pair(x, 0, 1 - y, part) + xr0[0, part, :].astype(F32)).astype(BF16)
-        begin("r", ys0.at[part], yr0.at[part], h_recv.at[0, h], to_y)
-    arrived(yr1.at[0], r_recv.at[1, 0])
-    for h, part in enumerate(halves):
+        begin("r", ys0.at[part], yr0.at[part], h_recv.at[0, q], to_y)
+        arrived(yr1.at[0, part], r_recv.at[1, 0, q])
         xs1[part, :] = (pair(1 - x, 1, y, part) + yr1[0, part, :].astype(F32)).astype(BF16)
-        begin("r", xs1.at[part], xr1.at[part], h_recv.at[1, h], to_x)
-
-    w_take(zk[0], 1 - y, x)
-    w_give(zk[0], 1 - y, x, to_x)
-    w_give(zk[0], 1 - y, x, to_c)
-    w_take(zk[1], y, 1 - x, far[1])
-    w_give(zk[1], y, 1 - x, to_y)
-    w_give(zk[1], y, 1 - x, to_c, far[1])
-    w_take(zk[0], y, 1 - x, far[0])
-    w_give(zk[0], y, 1 - x, to_c, far[0])
-    w_take(zk[1], 1 - y, x)
-    w_give(zk[1], 1 - y, x, to_c)
-
-    arrived(xr0.at[1], r_recv.at[0, 1])
-    arrived(yr1.at[1], r_recv.at[1, 1])
-    for h, part in enumerate(halves):
+        begin("r", xs1.at[part], xr1.at[part], h_recv.at[1, q], to_x)
+
+    def sum_z(q):
+        part = slices[q]
         for k, (first, second) in enumerate(((xr0, yr0), (yr1, xr1))):
-            arrived(second.at[part], h_recv.at[k, h])
+            arrived(first.at[1, part], r_recv.at[k, 1, q])
+            arrived(second.at[part], h_recv.at[k, q])
             total = (
                 pair(x, k, y, part) + first[1, part, :].astype(F32) + second[part, :].astype(F32)
             )
             zs[k, part, :] = total.astype(BF16)
-            begin("r", zs.at[k, part], zr.at[z, part], z_recv.at[h, z], device(zk[k], y, x, c), far[k])
+            begin("r", zs.at[k, part], zr.at[z, part], z_recv.at[q, z], device(zk[k], y, x, c), far[k])
 
             @pl.when(near[k])
             def _():
                 tot[part, :] = total
 
-    w_take(zk[0], 1 - y, 1 - x)
-    w_give(zk[0], 1 - y, 1 - x, to_c)
-    w_take(zk[1], 1 - y, 1 - x)
-    w_give(zk[1], 1 - y, 1 - x, to_c)
+    def sum_owner(q):
+        part = slices[q]
+
+        @pl.when(home)
+        def _():
+            total = tot[part, :]
+            for zz in others_z:
+                arrived(zr.at[zz, part], z_recv.at[q, zz])
+                total = total + zr[zz, part, :].astype(F32)
+            fin[c, part, :] = total.astype(BF16)
+
+        begin("r", fin.at[c, part], fin.at[c, part], f_recv.at[q, c], to_x, home)
+        begin("r", fin.at[c, part], fin.at[c, part], f_recv.at[q, c], to_c, home)
+
+    def other(q, u, k, yy):
+        zz = u + 2 * k
+        own = jnp.logical_and(zz == z, yy == y)
+        w_give(zz, yy, c, q, to_c, jnp.logical_not(own))
+
+    def gather_first(q):
+        for k, order in ((0, (to_y, to_x)), (1, (to_x, to_y))):
+            w_take(zk[k], y, c, q, far[k])
+            for dev in order:
+                w_give(zk[k], y, c, q, dev, far[k] if dev is to_x else None)
+            other(q, x, k, y)
+
+    def gather_second(q):
+        w_take(zk[0], 1 - y, c, q)
+        w_give(zk[0], 1 - y, c, q, to_x)
+        w_take(zk[1] + 1 - 2 * x, y, c, q, zk[1] + 1 - 2 * x != z)
+        w_give(zk[1] + 1 - 2 * x, y, c, q, to_y)
+        other(q, x, 0, 1 - y)
+        other(q, 1 - x, 1, y)
+        w_take(zk[0] + 1 - 2 * x, y, c, q, zk[0] + 1 - 2 * x != z)
+        other(q, 1 - x, 0, y)
+        w_take(zk[1], 1 - y, c, q)
+        other(q, x, 1, 1 - y)
+
+    def gather_last(q):
+        for k in (0, 1):
+            w_take(zk[k] + 1 - 2 * x, 1 - y, c, q)
+            other(q, 1 - x, k, 1 - y)
+
+    def gather_end(q):
+        for zz in range(4):
+            for yy in (0, 1):
+                own = jnp.logical_and(zz == z, yy == y)
+                w_take(zz, yy, 1 - c, q, jnp.logical_not(own))
+
     for k in (0, 1):
-        zz = 1 - c + 2 * k
-        for yy in (0, 1):
-            mine = jnp.logical_and(zz == z, yy == y)
-            for t in (0, 1):
-                w_take(zz, yy, t, jnp.logical_not(mine))
+        arrived(crecv.at[pl.ds(2 * k * region, 2 * region)], c_recv.at[k])
+
+    sum_first(0)
+    sum_first(1)
+    gather_first(0)
+    sum_second(0)
+    sum_first(2)
+    gather_first(1)
+    gather_second(0)
+    sum_second(1)
+    sum_z(0)
+    gather_first(2)
+    sum_second(2)
+    gather_second(1)
+    sum_z(1)
+    gather_last(0)
+    gather_second(2)
+    sum_z(2)
+    gather_last(1)
+    sum_owner(0)
+    gather_last(2)
+    sum_owner(1)
+    sum_owner(2)
+    gather_end(0)
+    gather_end(1)
+    gather_end(2)
 
     wide_route = jnp.concatenate([scale] * 3, axis=1)
 
@@ -232,35 +273,22 @@
         grad_hidden = grad_hidden + jnp.dot(gf[:, at], w, preferred_element_type=F32)
         return grad_hidden, route
 
-    grad_hidden, route = lax.fori_loop(
-        0, chunks, outputs,
-        (jnp.zeros((slots, 2 * LANES), F32), jnp.zeros((slots, LANES), F32)),
-    )
+    carry = (jnp.zeros((slots, 2 * LANES), F32), jnp.zeros((slots, LANES), F32))
+    carry = lax.fori_loop(0, chunks // 2, outputs, carry)
+    for q, part in enumerate(slices):
+        arrived(fin.at[c, part], f_recv.at[q, c], away)
+        begin("r", fin.at[c, part], fin.at[c, part], f_recv.at[q, c], to_c, away)
+    grad_hidden, route = lax.fori_loop(chunks // 2, chunks, outputs, carry)
     grad_route[...] = jnp.sum((live * route).T, axis=0, keepdims=True)
     gate, up, sig, activated = gates()
     grad_hidden = grad_hidden.T[:units, :]
     grad_gate_up[:units, :] = (grad_hidden * up * sig * (1.0 + gate * (1.0 - sig))).astype(BF16)
     grad_gate_up[units:, :] = (grad_hidden * activated).astype(BF16)
 
-    for h, part in enumerate(halves):
-        @pl.when(home)
-        def _():
-            total = tot[part, :]
-            for zz in others_z:
-                arrived(zr.at[zz, part], z_recv.at[h, zz])
-                total = total + zr[zz, part, :].astype(F32)
-            fin[x, part, :] = total
-
-        begin("r", fin.at[x, part], fin.at[x, part], f_recv.at[h, x], to_x, home)
-        begin("r", fin.at[x, part], fin.at[x, part], f_recv.at[h, x], to_c, home)
-    for h, part in enumerate(halves):
-        arrived(fin.at[1 - x, part], f_recv.at[h, 1 - x], home)
-        begin("r", fin.at[1 - x, part], fin.at[1 - x, part], f_recv.at[h, 1 - x], to_c, home)
-    for h, part in enumerate(halves):
-        arrived(fin.at[x, part], f_recv.at[h, x], away)
-        arrived(fin.at[1 - x, part], f_recv.at[h, 1 - x], away)
-    grad_down[:, :LANES] = fin[0]
-    grad_down[:, LANES:] = fin[1, :, :units - LANES]
+    for q, part in enumerate(slices):
+        arrived(fin.at[1 - c, part], f_recv.at[q, 1 - c])
+    grad_down[:, :LANES] = fin[0].astype(F32)
+    grad_down[:, LANES:] = fin[1].astype(F32)[:, :units - LANES]
 
     for copy, cond in pending:
         if cond is None:
@@ -309,7 +337,7 @@
             pltpu.VMEM((2, features, LANES), BF16),
             pltpu.VMEM((2, features, LANES), F32),
             pltpu.VMEM((2, features, LANES), BF16),
-            pltpu.VMEM((2, 2, region, LANES), BF16),
+            pltpu.VMEM((features, LANES), BF16),
             pltpu.VMEM((2,) + piece, BF16),
             pltpu.VMEM((2,) + piece, BF16),
             pltpu.VMEM(piece, BF16),
@@ -321,9 +349,9 @@
             pltpu.VMEM((2,) + piece, BF16),
             pltpu.VMEM((4,) + piece, BF16),
             pltpu.VMEM(piece, F32),
-            pltpu.VMEM((2,) + piece, F32),
-            dma((4,)), dma((2, 8)), dma((24,)), dma((2, 2)), dma((2, 2)), dma((2, 2)),
-            dma((24,)), dma((2, 4)), dma((2, 2)),
+            pltpu.VMEM((2,) + piece, BF16),
+            dma((4,)), dma((2, 8, SLICES)), dma((22 * SLICES,)), dma((2,)), dma((2, 2, SLICES)),
+            dma((2, SLICES)), dma((4 + 11 * SLICES,)), dma((SLICES, 4)), dma((SLICES, 2)),
         ],
         compiler_params=pltpu.CompilerParams(
             collective_id=0, has_side_effects=True, vmem_limit_bytes=58 * 2**20

time: 44 us -> 41.9 us (0.952)
  Pallas kernels: 42.6 us -> 40.4 us
    pallas_call x1, Pallas kernels: 41 us -> 38.8 us  [fused(): pl.pallas_call(kernel, out_shape=tuple((pltpu.VMEM(a.shape, a.dtype) for...]
where the time goes in v3:
time: 41.9 us; the launch traced here: 41.7 us
  Pallas kernels  40.4 us (96%)
  between operations  1.29 us (3%)
    pallas_call x1, Pallas kernels, fused(): pl.pallas_call(kernel, out_shape=tuple((pltpu.VMEM(a.shape, a.dtype) for...  38.8 us
    pallas_call x1, Pallas kernels, fused(): pl.pallas_call(place, out_shape=shapes, in_specs=[pl.BlockSpec(memory_spa...  1.63 us

profile of v3, /device:TPU:0, one launch (start us, length us, event | category | flops | bytes accessed | tf_op | source)
XLA Modules:
  0.0 41.7 jit_solution(3777182484784879801)
XLA Ops:
  1.3 38.8 %shard_map.84 = (bf16[256,4224]{1,0:T(8,128)(2,1)S(1)}, bf16[448,256]{1,0:T(8,128)(2,1)S(1)}, f32[1,256]{1,0:T(1,128)S(1)}, f32[528,224]{1,0:T(8,128)S(1)}) custom-call(bf16[448,256]{1,0:T(8,128)(2,1)} %bitcast.4, f32[1,256]{1,0:T(1,128)} %bitcast.6, s32[1]{0:T(128)S(6)} %copy.9.live_rows, bf16[528,224]{1,0:T(8,128)(2,1)} %weight.1, bf16[256,4224]{1,0:T(8,128)(2,1)} %out_grad.1), custom_call_target="tpu_custom_call" | custom-call | flops 1453326336 | bytes 6488064 | tf_op jit(solution)/shard_map/pallas_call | solution.py:325
  40.1 1.6 %shard_map.85 = (bf16[256,4224]{1,0:T(8,128)(2,1)}, bf16[448,256]{1,0:T(8,128)(2,1)}, f32[1,256]{1,0:T(1,128)}, f32[528,224]{1,0:T(8,128)}) custom-call(bf16[256,4224]{1,0:T(8,128)(2,1)S(1)} %get-tuple-element.12.refs_0_, bf16[448,256]{1,0:T(8,128)(2,1)S(1)} %get-tuple-element.13.refs_1_, f32[1,256]{1,0:T(1,128)S(1)} %get-tuple-element.14.refs_2_, ...), custom_call_target="tpu_custom_call" | custom-call | tf_op jit(solution)/shard_map/pallas_call | solution.py:363

commit v4 on v3

--- a/solution.py
+++ b/solution.py
@@ -145,6 +145,7 @@
     for q in range(SLICES):
         for zz in across:
             w_give(z, y, c, q, device(zz, y, x, c), home)
+        w_give(z, y, c, q, to_y, jnp.logical_or(home, z >= 2))
 
     def pair(u, k, yy, part):
         at = rows_of(u + 2 * k, yy, part)
@@ -206,14 +207,14 @@
         for k, order in ((0, (to_y, to_x)), (1, (to_x, to_y))):
             w_take(zk[k], y, c, q, far[k])
             for dev in order:
-                w_give(zk[k], y, c, q, dev, far[k] if dev is to_x else None)
+                w_give(zk[k], y, c, q, dev, far[k])
             other(q, x, k, y)
 
     def gather_second(q):
         w_take(zk[0], 1 - y, c, q)
         w_give(zk[0], 1 - y, c, q, to_x)
         w_take(zk[1] + 1 - 2 * x, y, c, q, zk[1] + 1 - 2 * x != z)
-        w_give(zk[1] + 1 - 2 * x, y, c, q, to_y)
+        w_give(zk[1] + 1 - 2 * x, y, c, q, to_y, zk[1] + 1 - 2 * x != z)
         other(q, x, 0, 1 - y)
         other(q, 1 - x, 1, y)
         w_take(zk[0] + 1 - 2 * x, y, c, q, zk[0] + 1 - 2 * x != z)
@@ -237,23 +238,23 @@
 
     sum_first(0)
     sum_first(1)
+    sum_second(0)
     gather_first(0)
-    sum_second(0)
     sum_first(2)
+    sum_second(1)
     gather_first(1)
+    sum_z(0)
     gather_second(0)
-    sum_second(1)
-    sum_z(0)
+    sum_second(2)
     gather_first(2)
-    sum_second(2)
-    gather_second(1)
     sum_z(1)
     gather_last(0)
-    gather_second(2)
+    gather_second(1)
     sum_z(2)
     gather_last(1)
+    gather_second(2)
+    gather_last(2)
     sum_owner(0)
-    gather_last(2)
     sum_owner(1)
     sum_owner(2)
     gather_end(0)

time: 41.9 us -> 41.1 us (0.981)
  the two profiles are of different devices: /device:TPU:0 before, /device:TPU:1 now
where the time goes in v4:
time: 41.1 us; the launch traced here: 41 us
  Pallas kernels  39.7 us (97%)
  between operations  1.29 us (3%)
    pallas_call x1, Pallas kernels, fused(): pl.pallas_call(kernel, out_shape=tuple((pltpu.VMEM(a.shape, a.dtype) for...  38.1 us
    pallas_call x1, Pallas kernels, fused(): pl.pallas_call(place, out_shape=shapes, in_specs=[pl.BlockSpec(memory_spa...  1.63 us

profile of v4, /device:TPU:1, one launch (start us, length us, event | category | flops | bytes accessed | tf_op | source)
XLA Modules:
  0.0 41.0 jit_solution(3355764294995905948)
XLA Ops:
  1.3 38.1 %shard_map.84 = (bf16[256,4224]{1,0:T(8,128)(2,1)S(1)}, bf16[448,256]{1,0:T(8,128)(2,1)S(1)}, f32[1,256]{1,0:T(1,128)S(1)}, f32[528,224]{1,0:T(8,128)S(1)}) custom-call(bf16[448,256]{1,0:T(8,128)(2,1)} %bitcast.4, f32[1,256]{1,0:T(1,128)} %bitcast.6, s32[1]{0:T(128)S(6)} %copy.9.live_rows, bf16[528,224]{1,0:T(8,128)(2,1)} %weight.1, bf16[256,4224]{1,0:T(8,128)(2,1)} %out_grad.1), custom_call_target="tpu_custom_call" | custom-call | flops 1453326336 | bytes 6488064 | tf_op jit(solution)/shard_map/pallas_call | solution.py:326
  39.3 1.6 %shard_map.85 = (bf16[256,4224]{1,0:T(8,128)(2,1)}, bf16[448,256]{1,0:T(8,128)(2,1)}, f32[1,256]{1,0:T(1,128)}, f32[528,224]{1,0:T(8,128)}) custom-call(bf16[256,4224]{1,0:T(8,128)(2,1)S(1)} %get-tuple-element.12.refs_0_, bf16[448,256]{1,0:T(8,128)(2,1)S(1)} %get-tuple-element.13.refs_1_, f32[1,256]{1,0:T(1,128)S(1)} %get-tuple-element.14.refs_2_, ...), custom_call_target="tpu_custom_call" | custom-call | tf_op jit(solution)/shard_map/pallas_call | solution.py:364
